TPU v7x, 256 devices: a whole 4x4x8 slice. The times are simulated.
256 devices in a mesh: inner: 32 (over z_hi, x, y), outer: 8 (over z_lo, core).
Axes of the slice: x: 4, y: 4, z: 8 (z_hi: 2, z_lo: 4; z = z_hi * 4 + z_lo), core: 2. Of those that a mesh axis runs over, the one named last changes fastest.
Arguments:
- queries: bfloat16 [131072, 8, 128], P(('inner', 'outer')), may hold values from -6 to 6
- key_tokens: bfloat16 [131072, 128], P(('inner', 'outer')), may hold values from -6 to 6
- value_tokens: bfloat16 [131072, 128], P(('inner', 'outer')), may hold values from -6 to 6
- out_grad: bfloat16 [131072, 8, 128], P(('inner', 'outer')), may hold values from -4 to 4
- forward_out: bfloat16 [131072, 8, 128], P(('inner', 'outer')), may hold values from -4 to 4
- log_norm: float32 [131072, 8], P(('inner', 'outer')), may hold values from 2 to 5
- block_list: int32 [1024, 8], P(('inner', 'outer')), may hold values from 0 to 1023, as said below
- block_live: int32 [1024], P(('inner', 'outer')), may hold values from 1 to 8
Outputs:
- query_grad: bfloat16 [131072, 8, 128], P(('inner', 'outer'))
- key_grad: bfloat16 [131072, 128], P(('inner', 'outer'))
- value_grad: bfloat16 [131072, 128], P(('inner', 'outer'))
Inputs may be any that keep to these rules, and one draw needn't show every extreme that they name: `block_list`: for query block b the first block_live[b] entries are distinct key block numbers k <= b, always including b itself, with k lying in the tokens of the device that holds b or of the 4 devices before it along inner+outer; the remaining entries equal b. Some query block uses all 8 entries.
All inputs are finite; a program needn't handle non-finite values.
Results may differ from a plain program's by a relative error of at most 0.0056.
Values may be sent and summed in bfloat16 or wider, within the bound.
No kernel may reach another device: no remote copies, remote signals or barrier semaphores. Data moves between devices by JAX's collectives and lax.ppermute only.
A program may use at most 64 MiB of HBM per device.

v0:
```python
import jax
import jax.numpy as jnp
from jax import lax
from jax.sharding import PartitionSpec as P

BLOCK = 128
REACH = 4


def passed_along(block, axis, distance):
    devices = range(lax.axis_size(axis))
    route = [(i - distance, i) for i in devices if i - distance in devices]
    return lax.ppermute(block, axis, route)


def slot_terms(
    window_blocks, window_base, qrows, grows, nrows, drows, query_pos, listed, live, score_scale
):
    head_size = qrows.shape[1]
    slot_index = listed - window_base
    picked = jnp.take(window_blocks, slot_index, axis=0)
    keys_picked = picked[:, :, :head_size]
    values_picked = picked[:, :, head_size:]
    scores = (
        jnp.einsum("rd,jcd->rjc", qrows, keys_picked, preferred_element_type=jnp.float32)
        * score_scale
    )
    key_pos = (
        listed[:, None] * picked.shape[1] + jnp.arange(picked.shape[1], dtype=jnp.int32)[None, :]
    )
    allowed = (key_pos[None, :, :] <= query_pos[:, None, None]) & live[None, :, None]
    weights = jnp.where(allowed, jnp.exp(scores - nrows[:, None, None]), jnp.float32(0.0))
    weights_low = weights.astype(jnp.bfloat16)
    weight_grad = jnp.einsum(
        "rd,jcd->rjc", grows, values_picked, preferred_element_type=jnp.float32
    )
    score_grad = (weights * (weight_grad - drows[:, None, None])).astype(jnp.bfloat16)
    query_part = (
        jnp.einsum("rjc,jcd->rd", score_grad, keys_picked, preferred_element_type=jnp.float32)
        * score_scale
    )
    key_part = (
        jnp.einsum("rjc,rd->jcd", score_grad, qrows, preferred_element_type=jnp.float32)
        * score_scale
    )
    value_part = jnp.einsum("rjc,rd->jcd", weights_low, grows, preferred_element_type=jnp.float32)
    return (query_part, slot_index, jnp.concatenate([key_part, value_part], axis=2))


def body(
    queries, key_tokens, value_tokens, out_grad, forward_out, log_norm, block_list, block_live
):
    local_tokens, head_count, head_size = queries.shape
    local_blocks = local_tokens // BLOCK
    row_count = BLOCK * head_count
    slot_total = block_list.shape[1]
    score_scale = head_size ** (-0.5)
    position = lax.axis_index(("inner", "outer"))
    key_value = jnp.concatenate([key_tokens, value_tokens], axis=1)
    moving = key_value
    pieces = [key_value]
    for repeat in range(REACH):
        moving = passed_along(moving, ("inner", "outer"), 1)
        pieces = [moving] + pieces
    window = jnp.stack(pieces)
    window_blocks = window.reshape((REACH + 1) * local_blocks, BLOCK, 2 * head_size)
    window_base = (position - REACH) * local_blocks
    delta = jnp.sum(out_grad.astype(jnp.float32) * forward_out.astype(jnp.float32), axis=2)
    delta_rows = delta.reshape(local_blocks, row_count)
    query_rows = queries.reshape(local_blocks, row_count, head_size)
    grad_rows = out_grad.reshape(local_blocks, row_count, head_size)
    norm_rows = log_norm.reshape(local_blocks, row_count)
    slot_order = jnp.arange(slot_total, dtype=jnp.int32)
    grads = jnp.zeros(((REACH + 1) * local_blocks, BLOCK, 2 * head_size), jnp.float32)

    def block_step(grads, inputs):
        block_index, qrows, grows, nrows, drows, listed, live_count = inputs
        global_block = position * local_blocks + block_index
        query_pos = global_block * BLOCK + jnp.arange(row_count, dtype=jnp.int32) // head_count
        query_part, slot_index, grad_part = slot_terms(
            window_blocks,
            window_base,
            qrows,
            grows,
            nrows,
            drows,
            query_pos,
            listed,
            slot_order < live_count,
            score_scale,
        )
        grads = grads.at[slot_index].add(grad_part)
        return (grads, query_part.astype(jnp.bfloat16))

    inputs = (
        jnp.arange(local_blocks, dtype=jnp.int32),
        query_rows,
        grad_rows,
        norm_rows,
        delta_rows,
        block_list,
        block_live,
    )
    grads, query_blocks = lax.scan(block_step, grads, inputs)
    grads = grads.reshape(REACH + 1, local_tokens, 2 * head_size)
    remote = grads[:REACH].astype(jnp.bfloat16)
    summed = grads[REACH]
    moving = remote[::-1]
    for reach_step in range(1, REACH + 1):
        moving = passed_along(moving, ("inner", "outer"), -1)
        summed = summed + moving[0].astype(jnp.float32)
        moving = moving[1:]
    query_grad = query_blocks.reshape(local_tokens, head_count, head_size)
    key_grad = summed[:, :head_size].astype(jnp.bfloat16)
    value_grad = summed[:, head_size:].astype(jnp.bfloat16)
    return (query_grad, key_grad, value_grad)


def solution(mesh):
    return jax.shard_map(
        body,
        mesh=mesh,
        in_specs=(
            P(("inner", "outer"), None, None),
            P(("inner", "outer"), None),
            P(("inner", "outer"), None),
            P(("inner", "outer"), None, None),
            P(("inner", "outer"), None, None),
            P(("inner", "outer"), None),
            P(("inner", "outer"), None),
            P(("inner", "outer")),
        ),
        out_specs=(
            P(("inner", "outer"), None, None),
            P(("inner", "outer"), None),
            P(("inner", "outer"), None),
        ),
        check_vma=False,
    )
```

profile of v0, /device:TPU:127, one launch (start us, length us, event | category | flops | bytes accessed | tf_op | source)
XLA Modules:
  0.0 194.9 jit_solution(79979655959379286)
XLA Ops:
  0.6 0.9 constant_dynamic-update-slice_fusion.1
  1.6 0.9 constant_dynamic-update-slice_fusion
  2.5 4.9 %collective-permute-start = (bf16[512,256]{1,0:T(8,128)(2,1)S(1)}, bf16[512,256]{1,0:T(8,128)(2,1)S(1)}, u32[]{:S(2)}, u32[]{:S(2)}) collective-permute-start(bf16[512,256]{1,0:T(8,128)(2,1)S(1)} %constant_dynamic-update-slice_fusion), channel_id=1, source_target_pairs={{0,1},{1,2},{2,3},{3,4},{4,5},{5,6},{6,7},{7,8},{8,9},{9,10},{10,1... | collective-permute-start | bytes 786440 | tf_op jit(solution)/shard_map/ppermute | solution.py:13
  7.4 3.3 %collective-permute-done = bf16[512,256]{1,0:T(8,128)(2,1)S(1)} collective-permute-done((bf16[512,256]{1,0:T(8,128)(2,1)S(1)}, bf16[512,256]{1,0:T(8,128)(2,1)S(1)}, u32[]{:S(2)}, u32[]{:S(2)}) %collective-permute-start) | collective-permute-done | bytes 262176 | tf_op jit(solution)/shard_map/ppermute | solution.py:13
  10.7 9.8 %collective-permute-start.1 = (bf16[512,256]{1,0:T(8,128)(2,1)S(1)}, bf16[512,256]{1,0:T(8,128)(2,1)S(1)}, u32[]{:S(2)}, u32[]{:S(2)}) collective-permute-start(bf16[512,256]{1,0:T(8,128)(2,1)S(1)} %collective-permute-done), channel_id=1, source_target_pairs={{0,1},{1,2},{2,3},{3,4},{4,5},{5,6},{6,7},{7,8},{8,9},{9,10},{10,1... | collective-permute-start | bytes 786440 | tf_op jit(solution)/shard_map/ppermute | solution.py:13
  20.5 3.3 %collective-permute-done.1 = bf16[512,256]{1,0:T(8,128)(2,1)S(1)} collective-permute-done((bf16[512,256]{1,0:T(8,128)(2,1)S(1)}, bf16[512,256]{1,0:T(8,128)(2,1)S(1)}, u32[]{:S(2)}, u32[]{:S(2)}) %collective-permute-start.1) | collective-permute-done | bytes 262176 | tf_op jit(solution)/shard_map/ppermute | solution.py:13
  23.8 9.8 %collective-permute-start.2 = (bf16[512,256]{1,0:T(8,128)(2,1)S(1)}, bf16[512,256]{1,0:T(8,128)(2,1)S(1)}, u32[]{:S(2)}, u32[]{:S(2)}) collective-permute-start(bf16[512,256]{1,0:T(8,128)(2,1)S(1)} %collective-permute-done.1), channel_id=1, source_target_pairs={{0,1},{1,2},{2,3},{3,4},{4,5},{5,6},{6,7},{7,8},{8,9},{9,10},{10,1... | collective-permute-start | bytes 786440 | tf_op jit(solution)/shard_map/ppermute | solution.py:13
  33.6 3.3 %collective-permute-done.2 = bf16[512,256]{1,0:T(8,128)(2,1)S(1)} collective-permute-done((bf16[512,256]{1,0:T(8,128)(2,1)S(1)}, bf16[512,256]{1,0:T(8,128)(2,1)S(1)}, u32[]{:S(2)}, u32[]{:S(2)}) %collective-permute-start.2) | collective-permute-done | bytes 262176 | tf_op jit(solution)/shard_map/ppermute | solution.py:13
  36.9 9.8 %collective-permute-start.3 = (bf16[512,256]{1,0:T(8,128)(2,1)S(1)}, bf16[512,256]{1,0:T(8,128)(2,1)S(1)}, u32[]{:S(2)}, u32[]{:S(2)}) collective-permute-start(bf16[512,256]{1,0:T(8,128)(2,1)S(1)} %collective-permute-done.2), channel_id=1, source_target_pairs={{0,1},{1,2},{2,3},{3,4},{4,5},{5,6},{6,7},{7,8},{8,9},{9,10},{10,1... | collective-permute-start | bytes 786440 | tf_op jit(solution)/shard_map/ppermute | solution.py:13
  46.8 2.2 %multiply_reduce_fusion = f32[512,8]{1,0:T(8,128)S(1)} fusion(bf16[512,8,128]{2,1,0:T(8,128)(2,1)} %param.14, bf16[512,8,128]{2,1,0:T(8,128)(2,1)} %param.13), kind=kLoop, calls=%fused_computation.53 | loop fusion | flops 2093056 | bytes 2113536 | tf_op jit(solution)/shard_map/reduce_sum | solution.py:68
  50.0 0.7 bitcast_dynamic-update-slice_fusion.4
  50.8 0.7 bitcast_dynamic-update-slice_fusion.3
  51.5 0.7 bitcast_dynamic-update-slice_fusion.2
  52.9 0.7 bitcast_dynamic-update-slice_fusion
  53.6 1.8 broadcast_in_dim.44
  55.5 66.2 %while.15 = (s32[]{:T(128)}, f32[20,128,256]{2,1,0:T(8,128)}, bf16[4,1024,128]{2,1,0:T(8,128)(2,1)}, s32[4,8]{1,0:T(4,128)S(1)}, s32[]{:T(128)}, /*index=5*/s32[...) while((s32[]{:T(128)}, f32[20,128,256]{2,1,0:T(8,128)}, ...), condition=%wide.region_3.4_spmd.clone, body=%wide.region_1.3_spmd.clone.sunk | while | flops 1358048384 | bytes 31515704 | solution.py:104
  58.3 1.9 gather_fusion
  61.0 2.5 %fusion.64 = f32[8,128,128]{1,2,0:T(8,128)S(1)} fusion(f32[1024,8,128]{2,0,1:T(8,128)S(1)} %fusion.62, f32[1024]{0:T(1024)S(1)} %bitcast.114, s32[8,128]{1,0:T(8,128)S(1)} %iota_add_fusion.2, s32[1024]{0:T(1024)S(1)} %fusion.63, pred[8]{0:T(512)(128)(4,1)S(1)} %iota_compare_fusion.2, bf16[4,1024,128]{2,1,0:T(8,128)(2,1)} %get-tuple-element.364, ...), kind=kOutput, calls=%fused_computation.6.clone.1 | convolution fusion | flops 274726912 | bytes 4993036 | tf_op jit(solution)/shard_map/while/body/eval_jaxpr/rjc,rd->jcd/dot_general | solution.py:46
  63.5 2.9 %multiply_convert_fusion.2 = bf16[1024,8,128]{2,0,1:T(8,128)(2,1)S(1)} fusion(f32[1024,8,128]{2,0,1:T(8,128)S(1)} %fusion.62, f32[1024]{0:T(1024)S(1)} %bitcast.113, f32[1024]{0:T(1024)S(1)} %bitcast.115, s32[8,128]{1,0:T(8,128)S(1)} %iota_add_fusion.2, s32[1024]{0:T(1024)S(1)} %fusion.63, pred[8]{0:T(512)(128)(4,1)S(1)} %iota_compare_fusion.2, ...), kind=kOutput, calls=%fused_computation.3.clone.1 | convolution fusion | flops 276824064 | bytes 6832644 | tf_op jit(solution)/shard_map/while/body/eval_jaxpr/rd,jcd->rjc/dot_general | solution.py:34
  66.4 1.4 fusion.65
  68.7 3.2 %scatter_fusion = f32[20,128,256]{2,1,0:T(8,128)} fusion(f32[20,128,256]{2,1,0:T(8,128)} %get-tuple-element.339, s32[8]{0:T(128)S(1)} %fusion.61, f32[8,128,256]{2,1,0:T(8,128)S(1)} %copy.23), kind=kCustom, calls=%fused_computation.1.clone.clone.1 | custom fusion | flops 262144 | bytes 3145760 | tf_op jit(solution)/shard_map/while/body/eval_jaxpr/scatter-add | solution.py:92
  74.7 1.9 gather_fusion
  77.4 2.5 %fusion.64 = f32[8,128,128]{1,2,0:T(8,128)S(1)} fusion(f32[1024,8,128]{2,0,1:T(8,128)S(1)} %fusion.62, f32[1024]{0:T(1024)S(1)} %bitcast.114, s32[8,128]{1,0:T(8,128)S(1)} %iota_add_fusion.2, s32[1024]{0:T(1024)S(1)} %fusion.63, pred[8]{0:T(512)(128)(4,1)S(1)} %iota_compare_fusion.2, bf16[4,1024,128]{2,1,0:T(8,128)(2,1)} %get-tuple-element.364, ...), kind=kOutput, calls=%fused_computation.6.clone.1 | convolution fusion | flops 274726912 | bytes 4993036 | tf_op jit(solution)/shard_map/while/body/eval_jaxpr/rjc,rd->jcd/dot_general | solution.py:46
  79.9 2.8 %multiply_convert_fusion.2 = bf16[1024,8,128]{2,0,1:T(8,128)(2,1)S(1)} fusion(f32[1024,8,128]{2,0,1:T(8,128)S(1)} %fusion.62, f32[1024]{0:T(1024)S(1)} %bitcast.113, f32[1024]{0:T(1024)S(1)} %bitcast.115, s32[8,128]{1,0:T(8,128)S(1)} %iota_add_fusion.2, s32[1024]{0:T(1024)S(1)} %fusion.63, pred[8]{0:T(512)(128)(4,1)S(1)} %iota_compare_fusion.2, ...), kind=kOutput, calls=%fused_computation.3.clone.1 | convolution fusion | flops 276824064 | bytes 6832644 | tf_op jit(solution)/shard_map/while/body/eval_jaxpr/rd,jcd->rjc/dot_general | solution.py:34
  82.8 1.4 fusion.65
  85.1 3.6 %scatter_fusion = f32[20,128,256]{2,1,0:T(8,128)} fusion(f32[20,128,256]{2,1,0:T(8,128)} %get-tuple-element.339, s32[8]{0:T(128)S(1)} %fusion.61, f32[8,128,256]{2,1,0:T(8,128)S(1)} %copy.23), kind=kCustom, calls=%fused_computation.1.clone.clone.1 | custom fusion | flops 262144 | bytes 3145760 | tf_op jit(solution)/shard_map/while/body/eval_jaxpr/scatter-add | solution.py:92
  91.5 1.9 gather_fusion
  94.2 2.5 %fusion.64 = f32[8,128,128]{1,2,0:T(8,128)S(1)} fusion(f32[1024,8,128]{2,0,1:T(8,128)S(1)} %fusion.62, f32[1024]{0:T(1024)S(1)} %bitcast.114, s32[8,128]{1,0:T(8,128)S(1)} %iota_add_fusion.2, s32[1024]{0:T(1024)S(1)} %fusion.63, pred[8]{0:T(512)(128)(4,1)S(1)} %iota_compare_fusion.2, bf16[4,1024,128]{2,1,0:T(8,128)(2,1)} %get-tuple-element.364, ...), kind=kOutput, calls=%fused_computation.6.clone.1 | convolution fusion | flops 274726912 | bytes 4993036 | tf_op jit(solution)/shard_map/while/body/eval_jaxpr/rjc,rd->jcd/dot_general | solution.py:46
  96.7 2.8 %multiply_convert_fusion.2 = bf16[1024,8,128]{2,0,1:T(8,128)(2,1)S(1)} fusion(f32[1024,8,128]{2,0,1:T(8,128)S(1)} %fusion.62, f32[1024]{0:T(1024)S(1)} %bitcast.113, f32[1024]{0:T(1024)S(1)} %bitcast.115, s32[8,128]{1,0:T(8,128)S(1)} %iota_add_fusion.2, s32[1024]{0:T(1024)S(1)} %fusion.63, pred[8]{0:T(512)(128)(4,1)S(1)} %iota_compare_fusion.2, ...), kind=kOutput, calls=%fused_computation.3.clone.1 | convolution fusion | flops 276824064 | bytes 6832644 | tf_op jit(solution)/shard_map/while/body/eval_jaxpr/rd,jcd->rjc/dot_general | solution.py:34
  99.5 1.4 fusion.65
  101.9 3.2 %scatter_fusion = f32[20,128,256]{2,1,0:T(8,128)} fusion(f32[20,128,256]{2,1,0:T(8,128)} %get-tuple-element.339, s32[8]{0:T(128)S(1)} %fusion.61, f32[8,128,256]{2,1,0:T(8,128)S(1)} %copy.23), kind=kCustom, calls=%fused_computation.1.clone.clone.1 | custom fusion | flops 262144 | bytes 3145760 | tf_op jit(solution)/shard_map/while/body/eval_jaxpr/scatter-add | solution.py:92
  107.9 1.9 gather_fusion
  109.9 0.7 fusion.62
  110.7 2.5 %fusion.64 = f32[8,128,128]{1,2,0:T(8,128)S(1)} fusion(f32[1024,8,128]{2,0,1:T(8,128)S(1)} %fusion.62, f32[1024]{0:T(1024)S(1)} %bitcast.114, s32[8,128]{1,0:T(8,128)S(1)} %iota_add_fusion.2, s32[1024]{0:T(1024)S(1)} %fusion.63, pred[8]{0:T(512)(128)(4,1)S(1)} %iota_compare_fusion.2, bf16[4,1024,128]{2,1,0:T(8,128)(2,1)} %get-tuple-element.364, ...), kind=kOutput, calls=%fused_computation.6.clone.1 | convolution fusion | flops 274726912 | bytes 4993036 | tf_op jit(solution)/shard_map/while/body/eval_jaxpr/rjc,rd->jcd/dot_general | solution.py:46
  113.1 2.8 %multiply_convert_fusion.2 = bf16[1024,8,128]{2,0,1:T(8,128)(2,1)S(1)} fusion(f32[1024,8,128]{2,0,1:T(8,128)S(1)} %fusion.62, f32[1024]{0:T(1024)S(1)} %bitcast.113, f32[1024]{0:T(1024)S(1)} %bitcast.115, s32[8,128]{1,0:T(8,128)S(1)} %iota_add_fusion.2, s32[1024]{0:T(1024)S(1)} %fusion.63, pred[8]{0:T(512)(128)(4,1)S(1)} %iota_compare_fusion.2, ...), kind=kOutput, calls=%fused_computation.3.clone.1 | convolution fusion | flops 276824064 | bytes 6832644 | tf_op jit(solution)/shard_map/while/body/eval_jaxpr/rd,jcd->rjc/dot_general | solution.py:34
  116.0 1.4 fusion.65
  118.3 3.3 %scatter_fusion = f32[20,128,256]{2,1,0:T(8,128)} fusion(f32[20,128,256]{2,1,0:T(8,128)} %get-tuple-element.339, s32[8]{0:T(128)S(1)} %fusion.61, f32[8,128,256]{2,1,0:T(8,128)S(1)} %copy.23), kind=kCustom, calls=%fused_computation.1.clone.clone.1 | custom fusion | flops 262144 | bytes 3145760 | tf_op jit(solution)/shard_map/while/body/eval_jaxpr/scatter-add | solution.py:92
  121.6 1.7 slice.88
  123.4 1.9 collective-permute-start.4
  125.3 20.8 %collective-permute-done.4 = bf16[4,512,256]{2,1,0:T(8,128)(2,1)S(1)} collective-permute-done((bf16[4,512,256]{2,1,0:T(8,128)(2,1)S(1)}, bf16[4,512,256]{2,1,0:T(8,128)(2,1)S(1)}, u32[]{:S(2)}, u32[]{:S(2)}) %collective-permute-start.4) | collective-permute-done | bytes 1048608 | tf_op jit(solution)/shard_map/ppermute | solution.py:13
  146.2 1.9 collective-permute-start.5
  148.1 16.8 %collective-permute-done.5 = bf16[3,512,256]{2,1,0:T(8,128)(2,1)S(1)} collective-permute-done((bf16[3,512,256]{2,1,0:T(8,128)(2,1)S(1)}, bf16[3,512,256]{2,1,0:T(8,128)(2,1)S(1)}, u32[]{:S(2)}, u32[]{:S(2)}) %collective-permute-start.5) | collective-permute-done | bytes 786464 | tf_op jit(solution)/shard_map/ppermute | solution.py:13
  164.9 1.9 collective-permute-start.6
  166.9 14.0 %collective-permute-done.6 = bf16[2,512,256]{2,1,0:T(8,128)(2,1)S(1)} collective-permute-done((bf16[2,512,256]{2,1,0:T(8,128)(2,1)S(1)}, bf16[2,512,256]{2,1,0:T(8,128)(2,1)S(1)}, u32[]{:S(2)}, u32[]{:S(2)}) %collective-permute-start.6) | collective-permute-done | bytes 524320 | tf_op jit(solution)/shard_map/ppermute | solution.py:13
  180.9 1.9 collective-permute-start.7
  182.8 1.1 slice.47
  183.9 10.1 %collective-permute-done.7 = bf16[1,512,256]{2,1,0:T(8,128)(2,1)S(1)} collective-permute-done((bf16[1,512,256]{2,1,0:T(8,128)(2,1)S(1)}, bf16[1,512,256]{2,1,0:T(8,128)(2,1)S(1)}, u32[]{:S(2)}, u32[]{:S(2)}) %collective-permute-start.7) | collective-permute-done | bytes 262176 | tf_op jit(solution)/shard_map/ppermute | solution.py:13
  194.2 0.7 fusion.33
  (79 shorter events, 16.7 us)
Async XLA Ops:
  0.6 48.5 %copy-start.1 = (f32[512,8]{0,1:T(8,128)S(1)}, f32[512,8]{0,1:T(8,128)}, u32[]{:S(2)}) copy-start(f32[512,8]{0,1:T(8,128)} %param.15) | copy-start | bytes 49156
  2.5 8.2 %collective-permute-start = (bf16[512,256]{1,0:T(8,128)(2,1)S(1)}, bf16[512,256]{1,0:T(8,128)(2,1)S(1)}, u32[]{:S(2)}, u32[]{:S(2)}) collective-permute-start(bf16[512,256]{1,0:T(8,128)(2,1)S(1)} %constant_dynamic-update-slice_fusion), channel_id=1, source_target_pairs={{0,1},{1,2},{2,3},{3,4},{4,5},{5,6},{6,7},{7,8},{8,9},{9,10},{10,1... | collective-permute-start | bytes 786440 | tf_op jit(solution)/shard_map/ppermute | solution.py:13
  10.7 13.1 %collective-permute-start.1 = (bf16[512,256]{1,0:T(8,128)(2,1)S(1)}, bf16[512,256]{1,0:T(8,128)(2,1)S(1)}, u32[]{:S(2)}, u32[]{:S(2)}) collective-permute-start(bf16[512,256]{1,0:T(8,128)(2,1)S(1)} %collective-permute-done), channel_id=1, source_target_pairs={{0,1},{1,2},{2,3},{3,4},{4,5},{5,6},{6,7},{7,8},{8,9},{9,10},{10,1... | collective-permute-start | bytes 786440 | tf_op jit(solution)/shard_map/ppermute | solution.py:13
  23.8 13.1 %collective-permute-start.2 = (bf16[512,256]{1,0:T(8,128)(2,1)S(1)}, bf16[512,256]{1,0:T(8,128)(2,1)S(1)}, u32[]{:S(2)}, u32[]{:S(2)}) collective-permute-start(bf16[512,256]{1,0:T(8,128)(2,1)S(1)} %collective-permute-done.1), channel_id=1, source_target_pairs={{0,1},{1,2},{2,3},{3,4},{4,5},{5,6},{6,7},{7,8},{8,9},{9,10},{10,1... | collective-permute-start | bytes 786440 | tf_op jit(solution)/shard_map/ppermute | solution.py:13
  36.9 13.1 %collective-permute-start.3 = (bf16[512,256]{1,0:T(8,128)(2,1)S(1)}, bf16[512,256]{1,0:T(8,128)(2,1)S(1)}, u32[]{:S(2)}, u32[]{:S(2)}) collective-permute-start(bf16[512,256]{1,0:T(8,128)(2,1)S(1)} %collective-permute-done.2), channel_id=1, source_target_pairs={{0,1},{1,2},{2,3},{3,4},{4,5},{5,6},{6,7},{7,8},{8,9},{9,10},{10,1... | collective-permute-start | bytes 786440 | tf_op jit(solution)/shard_map/ppermute | solution.py:13
  49.4 6.0 %copy-start = (bf16[512,8,128]{2,1,0:T(8,128)(2,1)S(1)}, bf16[512,8,128]{2,1,0:T(8,128)(2,1)}, u32[]{:S(2)}) copy-start(bf16[512,8,128]{2,1,0:T(8,128)(2,1)} %param.10) | copy-start | bytes 3145732
  49.4 6.0 %copy-start.2 = (s32[4,8]{1,0:T(4,128)S(1)}, s32[4,8]{1,0:T(4,128)}, u32[]{:S(2)}) copy-start(s32[4,8]{1,0:T(4,128)} %param.16) | copy-start | bytes 388
  49.4 6.0 %copy-start.3 = (s32[4]{0:T(128)S(1)}, s32[4]{0:T(128)}, u32[]{:S(2)}) copy-start(s32[4]{0:T(128)} %param.17) | copy-start | bytes 52
  123.4 22.7 %collective-permute-start.4 = (bf16[4,512,256]{2,1,0:T(8,128)(2,1)S(1)}, bf16[4,512,256]{2,1,0:T(8,128)(2,1)S(1)}, u32[]{:S(2)}, u32[]{:S(2)}) collective-permute-start(bf16[4,512,256]{2,1,0:T(8,128)(2,1)S(1)} %rev.3), channel_id=1, source_target_pairs={{1,0},{2,1},{3,2},{4,3},{5,4},{6,5},{7,6},{8,7},{9,8},{10,9},{11,1... | collective-permute-start | bytes 3145736 | tf_op jit(solution)/shard_map/ppermute | solution.py:13
  146.2 18.7 %collective-permute-start.5 = (bf16[3,512,256]{2,1,0:T(8,128)(2,1)S(1)}, bf16[3,512,256]{2,1,0:T(8,128)(2,1)S(1)}, u32[]{:S(2)}, u32[]{:S(2)}) collective-permute-start(bf16[3,512,256]{2,1,0:T(8,128)(2,1)S(1)} %slice.65), channel_id=1, source_target_pairs={{1,0},{2,1},{3,2},{4,3},{5,4},{6,5},{7,6},{8,7},{9,8},{10,9},{11,1... | collective-permute-start | bytes 2359304 | tf_op jit(solution)/shard_map/ppermute | solution.py:13
  164.9 15.9 %collective-permute-start.6 = (bf16[2,512,256]{2,1,0:T(8,128)(2,1)S(1)}, bf16[2,512,256]{2,1,0:T(8,128)(2,1)S(1)}, u32[]{:S(2)}, u32[]{:S(2)}) collective-permute-start(bf16[2,512,256]{2,1,0:T(8,128)(2,1)S(1)} %slice.67), channel_id=1, source_target_pairs={{1,0},{2,1},{3,2},{4,3},{5,4},{6,5},{7,6},{8,7},{9,8},{10,9},{11,1... | collective-permute-start | bytes 1572872 | tf_op jit(solution)/shard_map/ppermute | solution.py:13
  180.9 13.1 %collective-permute-start.7 = (bf16[1,512,256]{2,1,0:T(8,128)(2,1)S(1)}, bf16[1,512,256]{2,1,0:T(8,128)(2,1)S(1)}, u32[]{:S(2)}, u32[]{:S(2)}) collective-permute-start(bf16[1,512,256]{2,1,0:T(8,128)(2,1)S(1)} %slice.69), channel_id=1, source_target_pairs={{1,0},{2,1},{3,2},{4,3},{5,4},{6,5},{7,6},{8,7},{9,8},{10,9},{11,1... | collective-permute-start | bytes 786440 | tf_op jit(solution)/shard_map/ppermute | solution.py:13
where the time goes:
time: 196 us; the launch traced here: 195 us
  waiting for transfers between devices  72.2 us (37%)
  starting transfers between devices  42 us (21%)
  matrix products  31.8 us (16%)
  local copies, waits for them, and re-layouts  25.6 us (13%)
  other arithmetic  19.5 us (10%)
  loops' own time  3.1 us (2%)
    ppermute x8, waiting for transfers between devices, passed_along(): return lax.ppermute(block, axis, route)  72.2 us
    ppermute x8, starting transfers between devices, passed_along(): return lax.ppermute(block, axis, route)  42 us
    scatter-add x4, other arithmetic, block_step(): grads = grads.at[slot_index].add(grad_part)  13.2 us
    dot_general x4, matrix products, slot_terms(): jnp.einsum('rd,jcd->rjc', grows, values_picked, preferred_element_type=jn...  11.4 us
    dot_general x4, matrix products, slot_terms(): jnp.einsum('rjc,rd->jcd', weights_low, grows, preferred_element_type=jnp....  9.85 us
    gather x4, local copies, waits for them, and re-layouts, slot_terms(): picked = jnp.take(window_blocks, slot_index, axis=0)  7.59 us
    dot_general x4, matrix products, slot_terms(): jnp.einsum('rjc,jcd->rd', score_grad, keys_picked, preferred_element_type...  5.69 us
    dynamic_slice x12, local copies, waits for them, and re-layouts, body(): grads, query_blocks = lax.scan(block_step, grads, inputs)  5.25 us
  transfers between devices with their start and end apart: 8, of which 8 were waited for; matrix products, arithmetic and copies ran while one was open for 2% of the time, Pallas kernels for 0%

commit v1 on v0

v1 whole, which is shorter than its diff:
```python
import functools

import jax
import jax.numpy as jnp
from jax import lax
from jax.experimental import pallas as pl
from jax.experimental.pallas import tpu as pltpu
from jax.sharding import PartitionSpec as P

BLOCK = 128
AXES = ("inner", "outer")
LOG2E = 1.4426950408889634
NT = (((1,), (1,)), ((), ()))
TN = (((0,), (0,)), ((), ()))
F32 = jnp.float32
BF16 = jnp.bfloat16


def ring_shift(block, distance):
    count = lax.axis_size(AXES)
    route = [(i, (i + distance) % count) for i in range(count)]
    return lax.ppermute(block, AXES, route)


def pair_swap(block):
    count = lax.axis_size(AXES)
    return lax.ppermute(block, AXES, [(i, i ^ 1) for i in range(count)])


def tile_terms(keys, values, qrows, grows, norm, delta, scale, mask=None):
    score = lax.dot_general(keys, qrows, NT, preferred_element_type=F32)
    dweight = lax.dot_general(values, grows, NT, preferred_element_type=F32)
    weight = jnp.exp2(score * (scale * LOG2E) - norm)
    if mask is not None:
        weight = jnp.where(mask, weight, 0.0)
    score_grad = (weight * (dweight - delta)).astype(BF16)
    value_part = jnp.dot(weight.astype(BF16), grows, preferred_element_type=F32)
    key_part = jnp.dot(score_grad, qrows, preferred_element_type=F32)
    query_part = lax.dot_general(keys, score_grad, TN, preferred_element_type=F32)
    return query_part, key_part, value_part


def listed_slots(position, list_ref, live_ref, low, high, visit):
    step = pl.program_id(0)
    local_blocks = pl.num_programs(0)
    own = position * local_blocks + step

    def one(slot, carry):
        block = list_ref[step, slot]
        back = position - block // local_blocks

        @pl.when((back >= low) & (back <= high) & (block != own))
        def _():
            visit(back, block % local_blocks)

        return carry

    lax.fori_loop(0, live_ref[step], one, 0)


def own_kernel(
    position_ref, list_ref, live_ref, q_ref, g_ref, o_ref, norm_ref, k_ref, v_ref,
    delta_ref, dq_ref, dk_ref, dv_ref, *, scale,
):
    step = pl.program_id(0)
    rows, head_size = q_ref.shape
    heads = rows // BLOCK

    @pl.when(step == 0)
    def _():
        dk_ref[...] = jnp.zeros_like(dk_ref)
        dv_ref[...] = jnp.zeros_like(dv_ref)

    product = g_ref[...].astype(F32) * o_ref[...].astype(F32)
    high = product.astype(BF16)
    low = (product - high.astype(F32)).astype(BF16)
    ones = jnp.ones((8, head_size), BF16)
    delta = lax.dot_general(ones, high, NT, preferred_element_type=F32)
    delta = delta + lax.dot_general(ones, low, NT, preferred_element_type=F32)
    delta_ref[0] = delta[:1]

    base = pl.multiple_of(step * BLOCK, BLOCK)
    pieces = 4
    width = rows // pieces
    tokens = BLOCK // pieces
    for piece in range(pieces):
        seen = tokens * (piece + 1)
        span = pl.ds(piece * width, width)
        keys = k_ref[pl.ds(base, seen), :]
        values = v_ref[pl.ds(base, seen), :]
        key_pos = lax.broadcasted_iota(jnp.int32, (seen, width), 0)
        row_pos = lax.broadcasted_iota(jnp.int32, (seen, width), 1)
        mask = key_pos <= piece * tokens + row_pos // heads
        dq, dk, dv = tile_terms(
            keys, values, q_ref[span, :], g_ref[span, :], norm_ref[0, :, span],
            delta_ref[0, :, span], scale, mask,
        )
        dq_ref[0, :, span] = dq
        dk_ref[pl.ds(base, seen), :] += dk * scale
        dv_ref[pl.ds(base, seen), :] += dv

    def visit(back, local):
        at = pl.ds(pl.multiple_of(local * BLOCK, BLOCK), BLOCK)
        dq, dk, dv = tile_terms(
            k_ref[at, :], v_ref[at, :], q_ref[...], g_ref[...], norm_ref[0], delta_ref[0], scale
        )
        dq_ref[0] += dq
        dk_ref[at, :] += dk * scale
        dv_ref[at, :] += dv

    listed_slots(position_ref[0], list_ref, live_ref, 0, 0, visit)


def far_kernel(
    position_ref, list_ref, live_ref, q_ref, g_ref, norm_ref, delta_ref, dq_in_ref,
    ka_ref, va_ref, kb_ref, vb_ref,
    dq_ref, dka_ref, dva_ref, dkb_ref, dvb_ref, k_all, v_all, dk_acc, dv_acc, dq_acc,
    *, scale, low, last,
):
    step = pl.program_id(0)
    count = ka_ref.shape[0]

    @pl.when(step == 0)
    def _():
        k_all[pl.ds(0, count), :] = ka_ref[...]
        k_all[pl.ds(count, count), :] = kb_ref[...]
        v_all[pl.ds(0, count), :] = va_ref[...]
        v_all[pl.ds(count, count), :] = vb_ref[...]
        dk_acc[...] = jnp.zeros_like(dk_acc)
        dv_acc[...] = jnp.zeros_like(dv_acc)

    dq_acc[...] = dq_in_ref[0]

    def visit(back, local):
        at = pl.ds(pl.multiple_of((back - low) * count + local * BLOCK, BLOCK), BLOCK)
        dq, dk, dv = tile_terms(
            k_all[at, :], v_all[at, :], q_ref[...], g_ref[...], norm_ref[0], delta_ref[0], scale
        )
        dq_acc[...] += dq
        dk_acc[at, :] += dk
        dv_acc[at, :] += dv

    listed_slots(position_ref[0], list_ref, live_ref, low, low + 1, visit)

    if last:
        dq_ref[...] = (dq_acc[...] * scale).T.astype(dq_ref.dtype)
    else:
        dq_ref[0] = dq_acc[...]

    @pl.when(step == pl.num_programs(0) - 1)
    def _():
        dka_ref[...] = (dk_acc[pl.ds(0, count), :] * scale).astype(BF16)
        dkb_ref[...] = (dk_acc[pl.ds(count, count), :] * scale).astype(BF16)
        dva_ref[...] = dv_acc[pl.ds(0, count), :].astype(BF16)
        dvb_ref[...] = dv_acc[pl.ds(count, count), :].astype(BF16)


def body(
    queries, key_tokens, value_tokens, out_grad, forward_out, log_norm, block_list, block_live
):
    local_tokens, heads, head_size = queries.shape
    local_blocks = local_tokens // BLOCK
    rows = BLOCK * heads
    scale = head_size ** (-0.5)
    position = lax.axis_index(AXES).astype(jnp.int32)
    odd = lax.axis_index("outer") % 2 == 1
    scalars = (position.reshape(1), block_list, block_live)
    q = queries.reshape(local_blocks * rows, head_size)
    g = out_grad.reshape(local_blocks * rows, head_size)
    o = forward_out.reshape(local_blocks * rows, head_size)
    norm = (log_norm * LOG2E).reshape(local_blocks, 1, rows)

    row_spec = pl.BlockSpec((rows, head_size), lambda i, *_: (i, 0))
    line_spec = pl.BlockSpec((1, 1, rows), lambda i, *_: (i, 0, 0))
    dq_spec = pl.BlockSpec((1, head_size, rows), lambda i, *_: (i, 0, 0))
    shard_spec = pl.BlockSpec((local_tokens, head_size), lambda i, *_: (0, 0))
    line_shape = jax.ShapeDtypeStruct((local_blocks, 1, rows), F32)
    dq_shape = jax.ShapeDtypeStruct((local_blocks, head_size, rows), F32)
    part_shape = jax.ShapeDtypeStruct((local_tokens, head_size), BF16)
    wide_shape = jax.ShapeDtypeStruct((local_tokens, head_size), F32)
    params = pltpu.CompilerParams(
        dimension_semantics=("arbitrary",), vmem_limit_bytes=32 * 1024 * 1024
    )

    def cost(slots):
        return pl.CostEstimate(
            flops=slots * 10 * rows * BLOCK * head_size,
            bytes_accessed=4 * 1024 * 1024,
            transcendentals=slots * rows * BLOCK,
        )

    def own_call():
        return pl.pallas_call(
            functools.partial(own_kernel, scale=scale),
            grid_spec=pltpu.PrefetchScalarGridSpec(
                num_scalar_prefetch=3,
                grid=(local_blocks,),
                in_specs=[row_spec, row_spec, row_spec, line_spec, shard_spec, shard_spec],
                out_specs=[line_spec, dq_spec, shard_spec, shard_spec],
            ),
            out_shape=[line_shape, dq_shape, wide_shape, wide_shape],
            compiler_params=params,
            cost_estimate=cost(8),
            name="own_shard",
        )(*scalars, q, g, o, norm, key_tokens, value_tokens)

    def far_call(dq, delta, ka, va, kb, vb, low, last):
        wide = pltpu.VMEM((2 * local_tokens, head_size), F32)
        narrow = pltpu.VMEM((2 * local_tokens, head_size), BF16)
        return pl.pallas_call(
            functools.partial(far_kernel, scale=scale, low=low, last=last),
            grid_spec=pltpu.PrefetchScalarGridSpec(
                num_scalar_prefetch=3,
                grid=(local_blocks,),
                in_specs=[row_spec, row_spec, line_spec, line_spec, dq_spec] + [shard_spec] * 4,
                out_specs=[row_spec if last else dq_spec] + [shard_spec] * 4,
                scratch_shapes=[narrow, narrow, wide, wide, pltpu.VMEM((head_size, rows), F32)],
            ),
            out_shape=[
                jax.ShapeDtypeStruct(q.shape, BF16) if last else dq_shape
            ] + [part_shape] * 4,
            compiler_params=params,
            cost_estimate=cost(6),
            name="far_shards" if last else "near_shards",
        )(*scalars, q, g, norm, delta, dq, ka, va, kb, vb)

    k2 = ring_shift(key_tokens, 2)
    v2 = ring_shift(value_tokens, 2)
    k4 = ring_shift(k2, 2)
    v4 = ring_shift(v2, 2)
    delta, dq, dk0, dv0 = own_call()
    k1 = pair_swap(jnp.where(odd, k2, key_tokens))
    v1 = pair_swap(jnp.where(odd, v2, value_tokens))
    dq, dk1, dv1, dk2, dv2 = far_call(dq, delta, k1, v1, k2, v2, 1, False)
    k3 = pair_swap(jnp.where(odd, k4, k2))
    v3 = pair_swap(jnp.where(odd, v4, v2))
    dq, dk3, dv3, dk4, dv4 = far_call(dq, delta, k3, v3, k4, v4, 3, True)

    def give_back(own, part1, part2, part3, part4):
        zero = jnp.zeros((), F32)
        other3 = pair_swap(part3).astype(F32)
        other1 = pair_swap(part1).astype(F32)
        far = (part4.astype(F32) + jnp.where(odd, other3, zero)).astype(BF16)
        relayed = ring_shift(far, -2).astype(F32)
        near = part2.astype(F32) + jnp.where(odd, other1, other3) + relayed
        arrived = ring_shift(near.astype(BF16), -2).astype(F32)
        return (own + jnp.where(odd, zero, other1) + arrived).astype(BF16)

    key_grad = give_back(dk0, dk1, dk2, dk3, dk4)
    value_grad = give_back(dv0, dv1, dv2, dv3, dv4)
    return dq.reshape(queries.shape), key_grad, value_grad


def solution(mesh):
    tokens = P(AXES, None)
    wide = P(AXES, None, None)
    return jax.shard_map(
        body,
        mesh=mesh,
        in_specs=(wide, tokens, tokens, wide, wide, tokens, tokens, P(AXES)),
        out_specs=(wide, tokens, tokens),
        check_vma=False,
    )
```

time: 196 us -> 76.5 us (0.39)
  the two profiles are of different devices: /device:TPU:127 before, /device:TPU:1 now
where the time goes in v1:
time: 76.5 us; the launch traced here: 77.9 us
  waiting for transfers between devices  26.4 us (35%)
  starting transfers between devices  21.4 us (28%)
  Pallas kernels  19.8 us (26%)
  local copies, waits for them, and re-layouts  7.11 us (9%)
  other arithmetic  2.43 us (3%)
    ppermute x8, waiting for transfers between devices, ring_shift(): return lax.ppermute(block, AXES, route)  25.8 us
    pallas_call x2, Pallas kernels, far_call(): pl.pallas_call(functools.partial(far_kernel, scale=scale, low=low, last=l...  12.9 us
    ppermute x8, starting transfers between devices, ring_shift(): return lax.ppermute(block, AXES, route)  12.8 us
    ppermute x8, starting transfers between devices, pair_swap(): return lax.ppermute(block, AXES, [(i, i ^ 1) for i in range(count)])  8.59 us
    pallas_call x1, Pallas kernels, own_call(): pl.pallas_call(functools.partial(own_kernel, scale=scale), grid_spec=pltp...  6.87 us
    unnamed x14, local copies, waits for them, and re-layouts  6.82 us
  transfers between devices with their start and end apart: 16, of which 7 were waited for; matrix products, arithmetic and copies ran while one was open for 3% of the time, Pallas kernels for 21%

profile of v1, /device:TPU:1, one launch (start us, length us, event | category | flops | bytes accessed | tf_op | source)
XLA Modules:
  0.0 77.9 jit_solution(7470841767721611280)
XLA Ops:
  0.6 2.5 %collective-permute-start.2 = (bf16[512,128]{1,0:T(8,128)(2,1)}, bf16[512,128]{1,0:T(8,128)(2,1)S(1)}, u32[]{:S(2)}, u32[]{:S(2)}) collective-permute-start(bf16[512,128]{1,0:T(8,128)(2,1)} %v_ref.1), channel_id=1, source_target_pairs={{0,2},{1,3},{2,4},{3,5},{4,6},{5,7},{6,8},{7,9},{8,10},{9,11},{10,... | collective-permute-start | bytes 393224 | tf_op jit(solution)/shard_map/ppermute | solution.py:22
  3.2 1.6 %collective-permute-start = (bf16[512,128]{1,0:T(8,128)(2,1)}, bf16[512,128]{1,0:T(8,128)(2,1)S(1)}, u32[]{:S(2)}, u32[]{:S(2)}) collective-permute-start(bf16[512,128]{1,0:T(8,128)(2,1)} %k_ref.1), channel_id=1, source_target_pairs={{0,2},{1,3},{2,4},{3,5},{4,6},{5,7},{6,8},{7,9},{8,10},{9,11},{10,... | collective-permute-start | bytes 393224 | tf_op jit(solution)/shard_map/ppermute | solution.py:22
  4.8 10.4 %collective-permute-done.2.vb_ref = bf16[512,128]{1,0:T(8,128)(2,1)S(1)} collective-permute-done((bf16[512,128]{1,0:T(8,128)(2,1)}, bf16[512,128]{1,0:T(8,128)(2,1)S(1)}, u32[]{:S(2)}, u32[]{:S(2)}) %collective-permute-start.2) | collective-permute-done | bytes 131104 | tf_op jit(solution)/shard_map/ppermute | solution.py:22
  15.2 0.0 collective-permute-start.6
  15.2 2.8 %collective-permute-done.kb_ref = bf16[512,128]{1,0:T(8,128)(2,1)S(1)} collective-permute-done((bf16[512,128]{1,0:T(8,128)(2,1)}, bf16[512,128]{1,0:T(8,128)(2,1)S(1)}, u32[]{:S(2)}, u32[]{:S(2)}) %collective-permute-start) | collective-permute-done | bytes 131104 | tf_op jit(solution)/shard_map/ppermute | solution.py:22
  18.0 0.0 collective-permute-start.4
  18.0 6.4 %collective-permute-done.6.vb_ref = bf16[512,128]{1,0:T(8,128)(2,1)S(1)} collective-permute-done((bf16[512,128]{1,0:T(8,128)(2,1)S(1)}, bf16[512,128]{1,0:T(8,128)(2,1)S(1)}, u32[]{:S(2)}, u32[]{:S(2)}) %collective-permute-start.6) | collective-permute-done | bytes 131104 | tf_op jit(solution)/shard_map/ppermute | solution.py:22
  24.5 5.3 %collective-permute-start.3 = (bf16[512,128]{1,0:T(8,128)(2,1)S(1)}, bf16[512,128]{1,0:T(8,128)(2,1)S(1)}, u32[]{:S(2)}, u32[]{:S(2)}) collective-permute-start(bf16[512,128]{1,0:T(8,128)(2,1)S(1)} %get-tuple-element.32), channel_id=1, source_target_pairs={{0,1},{1,0},{2,3},{3,2},{4,5},{5,4},{6,7},{7,6},{8,9},{9,8},{10,11... | collective-permute-start | bytes 393224 | tf_op jit(solution)/shard_map/ppermute | solution.py:27
  29.8 0.0 collective-permute-done.4.kb_ref
  29.8 1.7 %collective-permute-start.1 = (bf16[512,128]{1,0:T(8,128)(2,1)S(1)}, bf16[512,128]{1,0:T(8,128)(2,1)S(1)}, u32[]{:S(2)}, u32[]{:S(2)}) collective-permute-start(bf16[512,128]{1,0:T(8,128)(2,1)S(1)} %get-tuple-element.34), channel_id=1, source_target_pairs={{0,1},{1,0},{2,3},{3,2},{4,5},{5,4},{6,7},{7,6},{8,9},{9,8},{10,11... | collective-permute-start | bytes 393224 | tf_op jit(solution)/shard_map/ppermute | solution.py:27
  31.5 0.7 broadcast_multiply_fusion
  32.2 0.1 copy.12
  32.3 0.2 reshape.30.norm_ref
  32.5 0.1 collective-permute-start.7
  32.6 0.5 collective-permute-start.5
  33.1 1.2 %copy-done = bf16[512,8,128]{2,1,0:T(8,128)(2,1)S(1)} copy-done((bf16[512,8,128]{2,1,0:T(8,128)(2,1)S(1)}, bf16[512,8,128]{2,1,0:T(8,128)(2,1)}, u32[]{:S(2)}) %copy-start) | copy-done | bytes 1048600
  34.3 1.2 %copy-done.1 = bf16[512,8,128]{2,1,0:T(8,128)(2,1)S(1)} copy-done((bf16[512,8,128]{2,1,0:T(8,128)(2,1)S(1)}, bf16[512,8,128]{2,1,0:T(8,128)(2,1)}, u32[]{:S(2)}) %copy-start.1) | copy-done | bytes 1048600
  35.6 0.9 %copy-done.2 = bf16[512,128]{1,0:T(8,128)(2,1)S(1)} copy-done((bf16[512,128]{1,0:T(8,128)(2,1)S(1)}, bf16[512,128]{1,0:T(8,128)(2,1)}, u32[]{:S(2)}) %copy-start.2) | copy-done | bytes 131096
  36.5 0.9 %copy-done.3 = bf16[512,128]{1,0:T(8,128)(2,1)S(1)} copy-done((bf16[512,128]{1,0:T(8,128)(2,1)S(1)}, bf16[512,128]{1,0:T(8,128)(2,1)}, u32[]{:S(2)}) %copy-start.3) | copy-done | bytes 131096
  37.4 0.7 copy-done.4
  38.0 0.7 copy-done.5
  38.7 1.2 %copy-done.6 = bf16[512,8,128]{2,1,0:T(8,128)(2,1)S(1)} copy-done((bf16[512,8,128]{2,1,0:T(8,128)(2,1)S(1)}, bf16[512,8,128]{2,1,0:T(8,128)(2,1)}, u32[]{:S(2)}) %copy-start.6) | copy-done | bytes 1048600
  39.9 6.9 %own_shard.1 = (f32[4,1,1024]{2,1,0:T(1,128)S(1)}, f32[4,128,1024]{2,1,0:T(8,128)S(1)}, f32[512,128]{1,0:T(8,128)S(1)}, f32[512,128]{1,0:T(8,128)S(1)}) custom-call(s32[1]{0:T(128)} %bitcast.position_ref, s32[4,8]{1,0:T(4,128)S(1)} %copy-done.4, s32[4]{0:T(128)S(1)} %copy-done.5, bf16[4096,128]{1,0:T(8,128)(2,1)S(1)} %bitcast.5, ...), custom_call_target="tpu_custom_call" | custom-call | flops 1342177280 | bytes 4194304 | tf_op jit(solution)/shard_map/own_shard/pallas_call | solution.py:193
  46.8 0.0 collective-permute-done.3.va_ref
  46.8 0.0 collective-permute-done.1.ka_ref
  46.8 9.8 %near_shards.1 = (f32[4,128,1024]{2,1,0:T(8,128)S(1)}, bf16[512,128]{1,0:T(8,128)(2,1)S(1)}, bf16[512,128]{1,0:T(8,128)(2,1)S(1)}, bf16[512,128]{1,0:T(8,128)(2,1)S(1)}, bf16[512,128]{1,0:T(8,128)(2,1)S(1)}) custom-call(s32[1]{0:T(128)} %bitcast.position_ref, s32[4,8]{1,0:T(4,128)S(1)} %copy-done.4, s32[4]{0:T(128)S(1)} %copy-done.5, ...), custom_call_target="tpu_custom_call" | custom-call | flops 1006632960 | bytes 4194304 | tf_op jit(solution)/shard_map/near_shards/pallas_call | solution.py:210
  56.6 0.0 collective-permute-done.7.va_ref
  56.6 0.0 collective-permute-done.5.ka_ref
  56.6 3.2 %far_shards.1 = (bf16[4096,128]{1,0:T(8,128)(2,1)}, bf16[512,128]{1,0:T(8,128)(2,1)S(1)}, bf16[512,128]{1,0:T(8,128)(2,1)S(1)}, bf16[512,128]{1,0:T(8,128)(2,1)S(1)}, bf16[512,128]{1,0:T(8,128)(2,1)S(1)}) custom-call(s32[1]{0:T(128)} %bitcast.position_ref, s32[4,8]{1,0:T(4,128)S(1)} %copy-done.4, s32[4]{0:T(128)S(1)} %copy-done.5, ...), custom_call_target="tpu_custom_call" | custom-call | flops 1006632960 | bytes 4194304 | tf_op jit(solution)/shard_map/far_shards/pallas_call | solution.py:210
  59.8 0.0 collective-permute-start.9
  59.8 0.5 collective-permute-start.13
  60.3 0.0 collective-permute-start.8
  60.3 0.5 collective-permute-start.12
  60.8 0.3 collective-permute-done.9
  61.2 0.1 collective-permute-start.10
  61.3 0.0 collective-permute-done.13
  61.4 0.1 collective-permute-start.14
  61.5 0.2 collective-permute-done.8
  61.6 4.6 %collective-permute-done.10 = bf16[512,128]{1,0:T(8,128)(2,1)S(1)} collective-permute-done((bf16[512,128]{1,0:T(8,128)(2,1)S(1)}, bf16[512,128]{1,0:T(8,128)(2,1)S(1)}, u32[]{:S(2)}, u32[]{:S(2)}) %collective-permute-start.10) | collective-permute-done | bytes 131104 | tf_op jit(solution)/shard_map/ppermute | solution.py:22
  66.2 0.1 fusion.5
  66.3 5.8 %collective-permute-start.11 = (bf16[512,128]{1,0:T(8,128)(2,1)S(1)}, bf16[512,128]{1,0:T(8,128)(2,1)S(1)}, u32[]{:S(2)}, u32[]{:S(2)}) collective-permute-start(bf16[512,128]{1,0:T(8,128)(2,1)S(1)} %fusion.5), channel_id=1, source_target_pairs={{0,254},{1,255},{2,0},{3,1},{4,2},{5,3},{6,4},{7,5},{8,6},{9,7},{1... | collective-permute-start | bytes 393224 | tf_op jit(solution)/shard_map/ppermute | solution.py:22
  72.0 0.0 collective-permute-done.12
  72.0 0.1 fusion.13
  72.1 2.7 %collective-permute-start.15 = (bf16[512,128]{1,0:T(8,128)(2,1)S(1)}, bf16[512,128]{1,0:T(8,128)(2,1)S(1)}, u32[]{:S(2)}, u32[]{:S(2)}) collective-permute-start(bf16[512,128]{1,0:T(8,128)(2,1)S(1)} %fusion.13), channel_id=1, source_target_pairs={{0,254},{1,255},{2,0},{3,1},{4,2},{5,3},{6,4},{7,5},{8,6},{9,7},{1... | collective-permute-start | bytes 393224 | tf_op jit(solution)/shard_map/ppermute | solution.py:22
  74.8 0.0 collective-permute-done.11
  74.9 0.7 fusion.2
  75.6 1.6 %collective-permute-done.15 = bf16[512,128]{1,0:T(8,128)(2,1)S(1)} collective-permute-done((bf16[512,128]{1,0:T(8,128)(2,1)S(1)}, bf16[512,128]{1,0:T(8,128)(2,1)S(1)}, u32[]{:S(2)}, u32[]{:S(2)}) %collective-permute-start.15) | collective-permute-done | bytes 131104 | tf_op jit(solution)/shard_map/ppermute | solution.py:22
  77.2 0.7 fusion.10
  (12 shorter events, 0.2 us)
Async XLA Ops:
  0.6 14.6 %collective-permute-start.2 = (bf16[512,128]{1,0:T(8,128)(2,1)}, bf16[512,128]{1,0:T(8,128)(2,1)S(1)}, u32[]{:S(2)}, u32[]{:S(2)}) collective-permute-start(bf16[512,128]{1,0:T(8,128)(2,1)} %v_ref.1), channel_id=1, source_target_pairs={{0,2},{1,3},{2,4},{3,5},{4,6},{5,7},{6,8},{7,9},{8,10},{9,11},{10,... | collective-permute-start | bytes 393224 | tf_op jit(solution)/shard_map/ppermute | solution.py:22
  3.2 14.8 %collective-permute-start = (bf16[512,128]{1,0:T(8,128)(2,1)}, bf16[512,128]{1,0:T(8,128)(2,1)S(1)}, u32[]{:S(2)}, u32[]{:S(2)}) collective-permute-start(bf16[512,128]{1,0:T(8,128)(2,1)} %k_ref.1), channel_id=1, source_target_pairs={{0,2},{1,3},{2,4},{3,5},{4,6},{5,7},{6,8},{7,9},{8,10},{9,11},{10,... | collective-permute-start | bytes 393224 | tf_op jit(solution)/shard_map/ppermute | solution.py:22
  15.2 9.2 %collective-permute-start.6 = (bf16[512,128]{1,0:T(8,128)(2,1)S(1)}, bf16[512,128]{1,0:T(8,128)(2,1)S(1)}, u32[]{:S(2)}, u32[]{:S(2)}) collective-permute-start(bf16[512,128]{1,0:T(8,128)(2,1)S(1)} %collective-permute-done.2.vb_ref), channel_id=1, source_target_pairs={{0,2},{1,3},{2,4},{3,5},{4,6},{5,7},{6,8},{7,9},{8,10},{9,11},{10,... | collective-permute-start | bytes 393224 | tf_op jit(solution)/shard_map/ppermute | solution.py:22
  18.0 11.8 %collective-permute-start.4 = (bf16[512,128]{1,0:T(8,128)(2,1)S(1)}, bf16[512,128]{1,0:T(8,128)(2,1)S(1)}, u32[]{:S(2)}, u32[]{:S(2)}) collective-permute-start(bf16[512,128]{1,0:T(8,128)(2,1)S(1)} %collective-permute-done.kb_ref), channel_id=1, source_target_pairs={{0,2},{1,3},{2,4},{3,5},{4,6},{5,7},{6,8},{7,9},{8,10},{9,11},{10,... | collective-permute-start | bytes 393224 | tf_op jit(solution)/shard_map/ppermute | solution.py:22
  24.5 22.3 %collective-permute-start.3 = (bf16[512,128]{1,0:T(8,128)(2,1)S(1)}, bf16[512,128]{1,0:T(8,128)(2,1)S(1)}, u32[]{:S(2)}, u32[]{:S(2)}) collective-permute-start(bf16[512,128]{1,0:T(8,128)(2,1)S(1)} %get-tuple-element.32), channel_id=1, source_target_pairs={{0,1},{1,0},{2,3},{3,2},{4,5},{5,4},{6,7},{7,6},{8,9},{9,8},{10,11... | collective-permute-start | bytes 393224 | tf_op jit(solution)/shard_map/ppermute | solution.py:27
  29.8 17.0 %collective-permute-start.1 = (bf16[512,128]{1,0:T(8,128)(2,1)S(1)}, bf16[512,128]{1,0:T(8,128)(2,1)S(1)}, u32[]{:S(2)}, u32[]{:S(2)}) collective-permute-start(bf16[512,128]{1,0:T(8,128)(2,1)S(1)} %get-tuple-element.34), channel_id=1, source_target_pairs={{0,1},{1,0},{2,3},{3,2},{4,5},{5,4},{6,7},{7,6},{8,9},{9,8},{10,11... | collective-permute-start | bytes 393224 | tf_op jit(solution)/shard_map/ppermute | solution.py:27
  32.5 24.1 %collective-permute-start.7 = (bf16[512,128]{1,0:T(8,128)(2,1)S(1)}, bf16[512,128]{1,0:T(8,128)(2,1)S(1)}, u32[]{:S(2)}, u32[]{:S(2)}) collective-permute-start(bf16[512,128]{1,0:T(8,128)(2,1)S(1)} %get-tuple-element.31), channel_id=1, source_target_pairs={{0,1},{1,0},{2,3},{3,2},{4,5},{5,4},{6,7},{7,6},{8,9},{9,8},{10,11... | collective-permute-start | bytes 393224 | tf_op jit(solution)/shard_map/ppermute | solution.py:27
  32.6 24.0 %collective-permute-start.5 = (bf16[512,128]{1,0:T(8,128)(2,1)S(1)}, bf16[512,128]{1,0:T(8,128)(2,1)S(1)}, u32[]{:S(2)}, u32[]{:S(2)}) collective-permute-start(bf16[512,128]{1,0:T(8,128)(2,1)S(1)} %get-tuple-element.33), channel_id=1, source_target_pairs={{0,1},{1,0},{2,3},{3,2},{4,5},{5,4},{6,7},{7,6},{8,9},{9,8},{10,11... | collective-permute-start | bytes 393224 | tf_op jit(solution)/shard_map/ppermute | solution.py:27
  33.1 1.2 %copy-start = (bf16[512,8,128]{2,1,0:T(8,128)(2,1)S(1)}, bf16[512,8,128]{2,1,0:T(8,128)(2,1)}, u32[]{:S(2)}) copy-start(bf16[512,8,128]{2,1,0:T(8,128)(2,1)} %param.8) | copy-start | bytes 3145732
  34.3 1.2 %copy-start.1 = (bf16[512,8,128]{2,1,0:T(8,128)(2,1)S(1)}, bf16[512,8,128]{2,1,0:T(8,128)(2,1)}, u32[]{:S(2)}) copy-start(bf16[512,8,128]{2,1,0:T(8,128)(2,1)} %param.11) | copy-start | bytes 3145732
  35.6 0.9 %copy-start.2 = (bf16[512,128]{1,0:T(8,128)(2,1)S(1)}, bf16[512,128]{1,0:T(8,128)(2,1)}, u32[]{:S(2)}) copy-start(bf16[512,128]{1,0:T(8,128)(2,1)} %k_ref.1) | copy-start | bytes 393220
  36.5 0.9 %copy-start.3 = (bf16[512,128]{1,0:T(8,128)(2,1)S(1)}, bf16[512,128]{1,0:T(8,128)(2,1)}, u32[]{:S(2)}) copy-start(bf16[512,128]{1,0:T(8,128)(2,1)} %v_ref.1) | copy-start | bytes 393220
  37.4 0.7 copy-start.4
  38.0 0.7 copy-start.5
  38.7 1.2 %copy-start.6 = (bf16[512,8,128]{2,1,0:T(8,128)(2,1)S(1)}, bf16[512,8,128]{2,1,0:T(8,128)(2,1)}, u32[]{:S(2)}) copy-start(bf16[512,8,128]{2,1,0:T(8,128)(2,1)} %param.12) | copy-start | bytes 3145732
  59.8 1.3 %collective-permute-start.9 = (bf16[512,128]{1,0:T(8,128)(2,1)S(1)}, bf16[512,128]{1,0:T(8,128)(2,1)S(1)}, u32[]{:S(2)}, u32[]{:S(2)}) collective-permute-start(bf16[512,128]{1,0:T(8,128)(2,1)S(1)} %get-tuple-element.24), channel_id=1, source_target_pairs={{0,1},{1,0},{2,3},{3,2},{4,5},{5,4},{6,7},{7,6},{8,9},{9,8},{10,11... | collective-permute-start | bytes 393224 | tf_op jit(solution)/shard_map/ppermute | solution.py:27
  59.8 1.5 %collective-permute-start.13 = (bf16[512,128]{1,0:T(8,128)(2,1)S(1)}, bf16[512,128]{1,0:T(8,128)(2,1)S(1)}, u32[]{:S(2)}, u32[]{:S(2)}) collective-permute-start(bf16[512,128]{1,0:T(8,128)(2,1)S(1)} %get-tuple-element.29), channel_id=1, source_target_pairs={{0,1},{1,0},{2,3},{3,2},{4,5},{5,4},{6,7},{7,6},{8,9},{9,8},{10,11... | collective-permute-start | bytes 393224 | tf_op jit(solution)/shard_map/ppermute | solution.py:27
  60.3 1.3 %collective-permute-start.8 = (bf16[512,128]{1,0:T(8,128)(2,1)S(1)}, bf16[512,128]{1,0:T(8,128)(2,1)S(1)}, u32[]{:S(2)}, u32[]{:S(2)}) collective-permute-start(bf16[512,128]{1,0:T(8,128)(2,1)S(1)} %get-tuple-element.22), channel_id=1, source_target_pairs={{0,1},{1,0},{2,3},{3,2},{4,5},{5,4},{6,7},{7,6},{8,9},{9,8},{10,11... | collective-permute-start | bytes 393224 | tf_op jit(solution)/shard_map/ppermute | solution.py:27
  60.3 11.7 %collective-permute-start.12 = (bf16[512,128]{1,0:T(8,128)(2,1)S(1)}, bf16[512,128]{1,0:T(8,128)(2,1)S(1)}, u32[]{:S(2)}, u32[]{:S(2)}) collective-permute-start(bf16[512,128]{1,0:T(8,128)(2,1)S(1)} %get-tuple-element.27), channel_id=1, source_target_pairs={{0,1},{1,0},{2,3},{3,2},{4,5},{5,4},{6,7},{7,6},{8,9},{9,8},{10,11... | collective-permute-start | bytes 393224 | tf_op jit(solution)/shard_map/ppermute | solution.py:27
  61.2 5.0 %collective-permute-start.10 = (bf16[512,128]{1,0:T(8,128)(2,1)S(1)}, bf16[512,128]{1,0:T(8,128)(2,1)S(1)}, u32[]{:S(2)}, u32[]{:S(2)}) collective-permute-start(bf16[512,128]{1,0:T(8,128)(2,1)S(1)} %fusion.7), channel_id=1, source_target_pairs={{0,254},{1,255},{2,0},{3,1},{4,2},{5,3},{6,4},{7,5},{8,6},{9,7},{1... | collective-permute-start | bytes 393224 | tf_op jit(solution)/shard_map/ppermute | solution.py:22
  61.4 10.7 %collective-permute-start.14 = (bf16[512,128]{1,0:T(8,128)(2,1)S(1)}, bf16[512,128]{1,0:T(8,128)(2,1)S(1)}, u32[]{:S(2)}, u32[]{:S(2)}) collective-permute-start(bf16[512,128]{1,0:T(8,128)(2,1)S(1)} %fusion.15), channel_id=1, source_target_pairs={{0,254},{1,255},{2,0},{3,1},{4,2},{5,3},{6,4},{7,5},{8,6},{9,7},{1... | collective-permute-start | bytes 393224 | tf_op jit(solution)/shard_map/ppermute | solution.py:22
  66.3 8.6 %collective-permute-start.11 = (bf16[512,128]{1,0:T(8,128)(2,1)S(1)}, bf16[512,128]{1,0:T(8,128)(2,1)S(1)}, u32[]{:S(2)}, u32[]{:S(2)}) collective-permute-start(bf16[512,128]{1,0:T(8,128)(2,1)S(1)} %fusion.5), channel_id=1, source_target_pairs={{0,254},{1,255},{2,0},{3,1},{4,2},{5,3},{6,4},{7,5},{8,6},{9,7},{1... | collective-permute-start | bytes 393224 | tf_op jit(solution)/shard_map/ppermute | solution.py:22
  72.1 5.0 %collective-permute-start.15 = (bf16[512,128]{1,0:T(8,128)(2,1)S(1)}, bf16[512,128]{1,0:T(8,128)(2,1)S(1)}, u32[]{:S(2)}, u32[]{:S(2)}) collective-permute-start(bf16[512,128]{1,0:T(8,128)(2,1)S(1)} %fusion.13), channel_id=1, source_target_pairs={{0,254},{1,255},{2,0},{3,1},{4,2},{5,3},{6,4},{7,5},{8,6},{9,7},{1... | collective-permute-start | bytes 393224 | tf_op jit(solution)/shard_map/ppermute | solution.py:22
